TPU v7x, 32 devices: a whole 2x2x4 slice. The times are simulated.
32 devices in a mesh: leaf: 8 (over z, x), sep: 4 (over y, core).
Axes of the slice: x: 2, y: 2, z: 4, core: 2. Of those that a mesh axis runs over, the one named last changes fastest.
Arguments:
- right_side: float32 [32768, 128], P(('leaf', 'sep')), may hold values from -6 to 6
- inverse_root: bfloat16 [8192, 8192], P(('leaf', 'sep')), may hold values from -1 to 3
- inverse_middle: bfloat16 [8192, 4096], P(('leaf', 'sep')), may hold values from -1 to 3
- inverse_lower: bfloat16 [16384, 4096], P(('leaf', 'sep')), may hold values from -1 to 3
- update_middle: bfloat16 [8192, 128], P(('leaf', 'sep')), may hold values from -0.09375 to 0.09375
- update_lower: bfloat16 [16384, 64], P(('leaf', 'sep')), may hold values from -0.09375 to 0.09375
- target_middle: int32 [32, 1], P(('leaf', 'sep')), may hold values from 0 to 31
- target_lower: int32 [32, 1], P(('leaf', 'sep')), may hold values from 0 to 63
Outputs:
- solution: float32 [32768, 128], P(('leaf', 'sep'))
All inputs are finite; a program needn't handle non-finite values.
Results may differ from a plain program's by a relative error of at most 0.0037.
Values may be sent and summed in bfloat16 or wider, within the bound.
A program may use at most 64 MiB of HBM per device.

v0:
```python
import jax
import jax.numpy as jnp
from jax import lax
from jax.sharding import PartitionSpec as P

BLOCK = 8


def from_partner(block, axis, distance):
    count = lax.axis_size(axis)
    route = []
    for low in range(count):
        high = low | 1 << distance
        if high != low and high < count:
            route += [(low, high), (high, low)]
    return lax.ppermute(block, axis, route)


def on_device(
    right_side,
    inverse_root,
    inverse_middle,
    inverse_lower,
    update_middle,
    update_lower,
    target_middle,
    target_lower,
):
    leaf_index = lax.axis_index("leaf")
    leaf_count = lax.axis_size("leaf")
    leaf_bits = leaf_count.bit_length() - 1
    dev_rows = inverse_root.shape[0]
    width = right_side.shape[1]
    root_side = right_side[:dev_rows]
    middle_side = right_side[dev_rows : 2 * dev_rows]
    lower_side = right_side[2 * dev_rows :]

    def collect(piece, depth_bits):
        panel = lax.all_gather(piece, "sep", axis=0, tiled=True)
        for bit_index in range(depth_bits):
            partner = from_partner(panel, "leaf", bit_index)
            upper = leaf_index >> bit_index & 1 == 1
            first = jnp.where(upper, partner, panel)
            second = jnp.where(upper, panel, partner)
            panel = jnp.concatenate([first, second], axis=0)
        return panel

    def apply_inverse(inverse, words, depth_bits):
        panel = collect(words, depth_bits)
        return jnp.dot(inverse, panel, preferred_element_type=jnp.float32)

    def halve_whole(current, depth_bits):
        for bit_index in reversed(range(depth_bits)):
            half = current.shape[0] // 2
            upper = leaf_index >> bit_index & 1 == 1
            keep = jnp.where(upper, current[half:], current[:half])
            give = jnp.where(upper, current[:half], current[half:])
            current = keep + from_partner(give, "leaf", bit_index)
        return current

    def reduce_slots(partial_value, depth_bits):
        current = halve_whole(partial_value, depth_bits)
        return lax.psum_scatter(current, "sep", scatter_dimension=0, tiled=True)

    def selector(targets, blocks):
        return (jnp.arange(blocks, dtype=jnp.int32)[:, None] == targets[0][None, :]).astype(
            jnp.float32
        )

    def place_slots(summed, targets, blocks):
        onehot = selector(targets, blocks)
        flat = summed.reshape(targets.shape[1], BLOCK * width)
        placed = jnp.dot(onehot, flat, precision=lax.Precision.HIGHEST)
        return placed.reshape(blocks * BLOCK, width)

    def pick_slots(table, targets, blocks):
        onehot = selector(targets, blocks)
        flat = table.astype(jnp.float32).reshape(blocks, BLOCK * width)
        picked = jnp.dot(onehot.T, flat, precision=lax.Precision.HIGHEST)
        return picked.reshape(targets.shape[1] * BLOCK, width).astype(jnp.bfloat16)

    contract_rows = (((0,), (0,)), ((), ()))
    lower_blocks = 2 * dev_rows // BLOCK
    middle_blocks = dev_rows // BLOCK
    lower_words = lower_side.astype(jnp.bfloat16)
    lower_values = apply_inverse(inverse_lower, lower_words, leaf_bits - 2)
    lower_partial = lax.dot_general(
        update_lower, lower_words, contract_rows, preferred_element_type=jnp.float32
    )
    lower_accum = place_slots(
        reduce_slots(lower_partial, leaf_bits - 2), target_lower, lower_blocks
    )
    middle_words = (middle_side - lower_accum[dev_rows:]).astype(jnp.bfloat16)
    middle_values = apply_inverse(inverse_middle, middle_words, leaf_bits - 1)
    middle_partial = lax.dot_general(
        update_middle, middle_words, contract_rows, preferred_element_type=jnp.float32
    )
    middle_accum = place_slots(
        reduce_slots(middle_partial, leaf_bits - 1), target_middle, middle_blocks
    )
    root_words = (root_side - (lower_accum[:dev_rows] + middle_accum)).astype(jnp.bfloat16)
    root_solution = apply_inverse(inverse_root, root_words, leaf_bits)
    root_rounded = root_solution.astype(jnp.bfloat16)
    middle_slots = collect(pick_slots(root_rounded, target_middle, middle_blocks), leaf_bits - 1)
    middle_solution = middle_values - jnp.dot(
        update_middle, middle_slots, preferred_element_type=jnp.float32
    )
    middle_rounded = middle_solution.astype(jnp.bfloat16)
    table = jnp.concatenate([root_rounded, middle_rounded], axis=0)
    lower_slots = collect(pick_slots(table, target_lower, lower_blocks), leaf_bits - 2)
    lower_solution = lower_values - jnp.dot(
        update_lower, lower_slots, preferred_element_type=jnp.float32
    )
    return jnp.concatenate([root_solution, middle_solution, lower_solution], axis=0)


def solution(mesh):
    in_specs = (
        P(("leaf", "sep"), None),
        P(("leaf", "sep"), None),
        P(("leaf", "sep"), None),
        P(("leaf", "sep"), None),
        P(("leaf", "sep"), None),
        P(("leaf", "sep"), None),
        P(("leaf", "sep"), None),
        P(("leaf", "sep"), None),
    )
    out_specs = P(("leaf", "sep"), None)
    return jax.shard_map(
        on_device, mesh=mesh, in_specs=in_specs, out_specs=out_specs, check_vma=False
    )
```

profile of v0, /device:TPU:0, one launch (start us, length us, event | category | flops | bytes accessed | tf_op | source)
XLA Modules:
  0.0 152.9 jit_solution(7578756123601498769)
XLA Ops:
  0.0 1.3 fusion.44
  1.3 3.0 %collective-permute-start = (f32[32,128]{1,0:T(8,128)S(1)}, f32[32,128]{1,0:T(8,128)S(1)}, u32[]{:S(2)}, u32[]{:S(2)}) collective-permute-start(f32[32,128]{1,0:T(8,128)S(1)} %slice_select_fusion.2), channel_id=1, source_target_pairs={{0,4},{4,0},{8,12},{12,8},{16,20},{20,16},{24,28},{28,24},{1,5},{5... | collective-permute-start | bytes 49160 | tf_op jit(solution)/shard_map/ppermute | solution.py:16
  5.0 1.2 dynamic-slice
  6.9 10.7 %all-reduce = f32[32,128]{1,0:T(8,128)S(1)} all-reduce(f32[32,128]{1,0:T(8,128)S(1)} %select_add_fusion.2), channel_id=2, replica_groups=mesh['leaf'=8,'sep'=4] {'sep'}, use_global_device_ids=true, to_apply=%region_0.1.clone | all-reduce | flops 4096 | bytes 32768
  17.7 0.9 subtract_convert_fusion.1
  18.6 1.1 convolution_bitcast_fusion
  19.7 1.6 %collective-permute-start.1 = (f32[64,128]{1,0:T(8,128)S(1)}, f32[64,128]{1,0:T(8,128)S(1)}, u32[]{:S(2)}, u32[]{:S(2)}) collective-permute-start(f32[64,128]{1,0:T(8,128)S(1)} %slice_select_fusion), channel_id=1, source_target_pairs={{0,8},{8,0},{4,12},{12,4},{16,24},{24,16},{20,28},{28,20},{1,9},{9... | collective-permute-start | bytes 98312 | tf_op jit(solution)/shard_map/ppermute | solution.py:16
  22.0 1.7 %collective-permute-done.1 = f32[64,128]{1,0:T(8,128)S(1)} collective-permute-done((f32[64,128]{1,0:T(8,128)S(1)}, f32[64,128]{1,0:T(8,128)S(1)}, u32[]{:S(2)}, u32[]{:S(2)}) %collective-permute-start.1) | collective-permute-done | bytes 32800 | tf_op jit(solution)/shard_map/ppermute | solution.py:16
  23.7 0.7 collective-permute-start.2
  24.4 3.1 %collective-permute-done.2 = f32[32,128]{1,0:T(8,128)S(1)} collective-permute-done((f32[32,128]{1,0:T(8,128)S(1)}, f32[32,128]{1,0:T(8,128)S(1)}, u32[]{:S(2)}, u32[]{:S(2)}) %collective-permute-start.2) | collective-permute-done | bytes 16416 | tf_op jit(solution)/shard_map/ppermute | solution.py:16
  27.5 10.1 %all-reduce.1 = f32[32,128]{1,0:T(8,128)S(1)} all-reduce(f32[32,128]{1,0:T(8,128)S(1)} %select_add_fusion.1), channel_id=3, replica_groups=mesh['leaf'=8,'sep'=4] {'sep'}, use_global_device_ids=true, to_apply=%region_1.2.clone | all-reduce | flops 4096 | bytes 32768
  37.7 0.9 subtract_convert_fusion
  38.7 5.8 %all_gather.15 = bf16[1024,128]{1,0:T(8,128)(2,1)S(1)} all-gather(bf16[256,128]{1,0:T(8,128)(2,1)S(1)} %subtract_convert_fusion), channel_id=1, replica_groups=mesh['leaf'=8,'sep'=4] {'sep'}, dimensions={0}, use_global_device_ids=true | all-gather | bytes 327680 | tf_op jit(solution)/shard_map/all_gather | solution.py:39
  44.5 0.7 collective-permute-start.3
  45.1 7.9 %collective-permute-done.3 = bf16[1024,128]{1,0:T(8,128)(2,1)S(1)} collective-permute-done((bf16[1024,128]{1,0:T(8,128)(2,1)S(1)}, bf16[1024,128]{1,0:T(8,128)(2,1)S(1)}, u32[]{:S(2)}, u32[]{:S(2)}) %collective-permute-start.3) | collective-permute-done | bytes 262176 | tf_op jit(solution)/shard_map/ppermute | solution.py:16
  53.1 1.6 %collective-permute-start.4 = (bf16[2048,128]{1,0:T(8,128)(2,1)S(1)}, bf16[2048,128]{1,0:T(8,128)(2,1)S(1)}, u32[]{:S(2)}, u32[]{:S(2)}) collective-permute-start(bf16[2048,128]{1,0:T(8,128)(2,1)S(1)} %pad_maximum_fusion.1), channel_id=1, source_target_pairs={{0,8},{8,0},{4,12},{12,4},{16,24},{24,16},{20,28},{28,20},{1,9},{9... | collective-permute-start | bytes 1572872 | tf_op jit(solution)/shard_map/ppermute | solution.py:16
  54.8 11.8 %collective-permute-done.4 = bf16[2048,128]{1,0:T(8,128)(2,1)S(1)} collective-permute-done((bf16[2048,128]{1,0:T(8,128)(2,1)S(1)}, bf16[2048,128]{1,0:T(8,128)(2,1)S(1)}, u32[]{:S(2)}, u32[]{:S(2)}) %collective-permute-start.4) | collective-permute-done | bytes 524320 | tf_op jit(solution)/shard_map/ppermute | solution.py:16
  66.6 0.2 broadcast_select_fusion.7
  66.8 1.1 pad_maximum_fusion
  67.8 2.6 %collective-permute-start.5 = (bf16[4096,128]{1,0:T(8,128)(2,1)}, bf16[4096,128]{1,0:T(8,128)(2,1)}, u32[]{:S(2)}, u32[]{:S(2)}) collective-permute-start(bf16[4096,128]{1,0:T(8,128)(2,1)} %pad_maximum_fusion), channel_id=1, source_target_pairs={{0,16},{16,0},{4,20},{20,4},{8,24},{24,8},{12,28},{28,12},{1,17},{... | collective-permute-start | bytes 3145736 | tf_op jit(solution)/shard_map/ppermute | solution.py:16
  70.4 5.8 %all_gather.16 = bf16[1024,128]{1,0:T(8,128)(2,1)S(1)} all-gather(bf16[256,128]{1,0:T(8,128)(2,1)S(1)} %subtract_convert_fusion.1), channel_id=1, replica_groups=mesh['leaf'=8,'sep'=4] {'sep'}, dimensions={0}, use_global_device_ids=true | all-gather | bytes 327680 | tf_op jit(solution)/shard_map/all_gather | solution.py:39
  76.2 0.7 collective-permute-start.6
  76.9 1.0 slice.81
  77.9 7.0 %collective-permute-done.6 = bf16[1024,128]{1,0:T(8,128)(2,1)} collective-permute-done((bf16[1024,128]{1,0:T(8,128)(2,1)S(1)}, bf16[1024,128]{1,0:T(8,128)(2,1)}, u32[]{:S(2)}, u32[]{:S(2)}) %collective-permute-start.6) | collective-permute-done | bytes 262176 | tf_op jit(solution)/shard_map/ppermute | solution.py:16
  84.9 1.1 broadcast_select_fusion.9
  85.9 0.7 copy-done.1
  86.7 0.8 pad_maximum_fusion.2
  87.5 1.6 %collective-permute-start.7 = (bf16[2048,128]{1,0:T(8,128)(2,1)}, bf16[2048,128]{1,0:T(8,128)(2,1)}, u32[]{:S(2)}, u32[]{:S(2)}) collective-permute-start(bf16[2048,128]{1,0:T(8,128)(2,1)} %pad_maximum_fusion.2), channel_id=1, source_target_pairs={{0,8},{8,0},{4,12},{12,4},{16,24},{24,16},{20,28},{28,20},{1,9},{9... | collective-permute-start | bytes 1572872 | tf_op jit(solution)/shard_map/ppermute | solution.py:16
  89.1 26.3 %collective-permute-done.5 = bf16[4096,128]{1,0:T(8,128)(2,1)} collective-permute-done((bf16[4096,128]{1,0:T(8,128)(2,1)}, bf16[4096,128]{1,0:T(8,128)(2,1)}, u32[]{:S(2)}, u32[]{:S(2)}) %collective-permute-start.5) | collective-permute-done | bytes 1048608 | tf_op jit(solution)/shard_map/ppermute | solution.py:16
  115.3 1.6 %broadcast_select_fusion.1 = (bf16[4096,128]{1,0:T(8,128)(2,1)S(1)}, bf16[4096,128]{1,0:T(8,128)(2,1)S(1)}) fusion(bf16[4096,128]{1,0:T(8,128)(2,1)} %collective-permute-done.5, pred[]{:T(512)S(6)} %eq.94, bf16[2048,128]{1,0:T(8,128)(2,1)S(1)} %get-tuple-element.12, bf16[2048,128]{1,0:T(8,128)(2,1)S(1)} %get-tuple-element.11), kind=kLoop, calls=%fused_computation.18 | loop fusion | flops 3145728 | bytes 4194305 | tf_op jit(solution)/shard_map/jit(_where)/select_n | solution.py:43
  117.0 2.2 %fusion.42 = (bf16[256,128]{0,1:T(8,128)(2,1)S(1)}, f32[256,128]{0,1:T(8,128)}) fusion(bf16[256,8192]{1,0:T(8,128)(2,1)S(1)} %copy-done.7, bf16[4096,128]{1,0:T(8,128)(2,1)S(1)} %get-tuple-element.6, bf16[4096,128]{1,0:T(8,128)(2,1)S(1)} %get-tuple-element.5), kind=kOutput, calls=%fused_computation.82 | convolution fusion | flops 541097984 | bytes 6488064 | tf_op jit(solution)/shard_map/dot_general | solution.py:50
  119.5 5.2 %all_gather.17 = bf16[32,128]{1,0:T(8,128)(2,1)S(1)} all-gather(bf16[8,128]{1,0:T(8,128)(2,1)S(1)} %convert_element_type.28), channel_id=1, replica_groups=mesh['leaf'=8,'sep'=4] {'sep'}, dimensions={0}, use_global_device_ids=true | all-gather | bytes 10240 | tf_op jit(solution)/shard_map/all_gather | solution.py:39
  124.6 0.7 collective-permute-start.8
  125.3 7.2 %all_gather.18 = bf16[2048,128]{1,0:T(8,128)(2,1)S(1)} all-gather(bf16[512,128]{1,0:T(8,128)(2,1)S(1)} %slice.81), channel_id=1, replica_groups=mesh['leaf'=8,'sep'=4] {'sep'}, dimensions={0}, use_global_device_ids=true | all-gather | bytes 655360 | tf_op jit(solution)/shard_map/all_gather | solution.py:39
  132.5 1.1 collective-permute-start.10
  133.6 0.7 collective-permute-start.9
  134.3 1.2 broadcast_select_fusion.5
  135.5 1.9 %collective-permute-done.9 = bf16[64,128]{1,0:T(8,128)(2,1)S(1)} collective-permute-done((bf16[64,128]{1,0:T(8,128)(2,1)S(1)}, bf16[64,128]{1,0:T(8,128)(2,1)S(1)}, u32[]{:S(2)}, u32[]{:S(2)}) %collective-permute-start.9) | collective-permute-done | bytes 16416 | tf_op jit(solution)/shard_map/ppermute | solution.py:16
  137.4 0.2 fusion.21
  137.6 0.9 fusion.43
  138.7 0.1 fusion.15
  138.9 5.2 %all_gather.19 = bf16[32,128]{1,0:T(8,128)(2,1)S(1)} all-gather(bf16[8,128]{1,0:T(8,128)(2,1)S(1)} %convert_element_type.30), channel_id=1, replica_groups=mesh['leaf'=8,'sep'=4] {'sep'}, dimensions={0}, use_global_device_ids=true | all-gather | bytes 10240 | tf_op jit(solution)/shard_map/all_gather | solution.py:39
  144.0 0.9 collective-permute-start.11
  144.9 1.8 %collective-permute-done.10 = bf16[2048,128]{1,0:T(8,128)(2,1)} collective-permute-done((bf16[2048,128]{1,0:T(8,128)(2,1)S(1)}, bf16[2048,128]{1,0:T(8,128)(2,1)}, u32[]{:S(2)}, u32[]{:S(2)}) %collective-permute-start.10) | collective-permute-done | bytes 524320 | tf_op jit(solution)/shard_map/ppermute | solution.py:16
  146.8 1.1 broadcast_select_fusion.3
  147.9 0.2 fusion.25
  148.1 3.8 %fusion.4 = f32[512,128]{0,1:T(8,128)S(1)} fusion(f32[128,512]{1,0:T(8,128)S(1)} %fusion.25, bf16[512,4096]{1,0:T(8,128)(2,1)} %param.11, bf16[2048,128]{1,0:T(8,128)(2,1)S(1)} %get-tuple-element.8, bf16[2048,128]{1,0:T(8,128)(2,1)S(1)} %get-tuple-element.7), kind=kOutput, calls=%fused_computation.5 | convolution fusion | flops 539033600 | bytes 5767168 | tf_op jit(solution)/shard_map/dot_general | solution.py:50
  152.0 1.0 copy.15
  (49 shorter events, 1.0 us)
Async XLA Ops:
  0.0 137.6 %copy-start = (bf16[256,4096]{1,0:T(8,128)(2,1)S(1)}, bf16[256,4096]{1,0:T(8,128)(2,1)}, u32[]{:S(2)}) copy-start(bf16[256,4096]{1,0:T(8,128)(2,1)} %param.10) | copy-start | bytes 6291460
  1.3 5.6 %collective-permute-start = (f32[32,128]{1,0:T(8,128)S(1)}, f32[32,128]{1,0:T(8,128)S(1)}, u32[]{:S(2)}, u32[]{:S(2)}) collective-permute-start(f32[32,128]{1,0:T(8,128)S(1)} %slice_select_fusion.2), channel_id=1, source_target_pairs={{0,4},{4,0},{8,12},{12,8},{16,20},{20,16},{24,28},{28,24},{1,5},{5... | collective-permute-start | bytes 49160 | tf_op jit(solution)/shard_map/ppermute | solution.py:16
  19.7 4.0 %collective-permute-start.1 = (f32[64,128]{1,0:T(8,128)S(1)}, f32[64,128]{1,0:T(8,128)S(1)}, u32[]{:S(2)}, u32[]{:S(2)}) collective-permute-start(f32[64,128]{1,0:T(8,128)S(1)} %slice_select_fusion), channel_id=1, source_target_pairs={{0,8},{8,0},{4,12},{12,4},{16,24},{24,16},{20,28},{28,20},{1,9},{9... | collective-permute-start | bytes 98312 | tf_op jit(solution)/shard_map/ppermute | solution.py:16
  23.7 3.8 %collective-permute-start.2 = (f32[32,128]{1,0:T(8,128)S(1)}, f32[32,128]{1,0:T(8,128)S(1)}, u32[]{:S(2)}, u32[]{:S(2)}) collective-permute-start(f32[32,128]{1,0:T(8,128)S(1)} %slice_select_fusion.1), channel_id=1, source_target_pairs={{0,4},{4,0},{8,12},{12,8},{16,20},{20,16},{24,28},{28,24},{1,5},{5... | collective-permute-start | bytes 49160 | tf_op jit(solution)/shard_map/ppermute | solution.py:16
  44.5 8.6 %collective-permute-start.3 = (bf16[1024,128]{1,0:T(8,128)(2,1)S(1)}, bf16[1024,128]{1,0:T(8,128)(2,1)S(1)}, u32[]{:S(2)}, u32[]{:S(2)}) collective-permute-start(bf16[1024,128]{1,0:T(8,128)(2,1)S(1)} %all_gather.15), channel_id=1, source_target_pairs={{0,4},{4,0},{8,12},{12,8},{16,20},{20,16},{24,28},{28,24},{1,5},{5... | collective-permute-start | bytes 786440 | tf_op jit(solution)/shard_map/ppermute | solution.py:16
  53.1 13.4 %collective-permute-start.4 = (bf16[2048,128]{1,0:T(8,128)(2,1)S(1)}, bf16[2048,128]{1,0:T(8,128)(2,1)S(1)}, u32[]{:S(2)}, u32[]{:S(2)}) collective-permute-start(bf16[2048,128]{1,0:T(8,128)(2,1)S(1)} %pad_maximum_fusion.1), channel_id=1, source_target_pairs={{0,8},{8,0},{4,12},{12,4},{16,24},{24,16},{20,28},{28,20},{1,9},{9... | collective-permute-start | bytes 1572872 | tf_op jit(solution)/shard_map/ppermute | solution.py:16
  67.8 47.5 %collective-permute-start.5 = (bf16[4096,128]{1,0:T(8,128)(2,1)}, bf16[4096,128]{1,0:T(8,128)(2,1)}, u32[]{:S(2)}, u32[]{:S(2)}) collective-permute-start(bf16[4096,128]{1,0:T(8,128)(2,1)} %pad_maximum_fusion), channel_id=1, source_target_pairs={{0,16},{16,0},{4,20},{20,4},{8,24},{24,8},{12,28},{28,12},{1,17},{... | collective-permute-start | bytes 3145736 | tf_op jit(solution)/shard_map/ppermute | solution.py:16
  76.2 1.6 %copy-start.3 = (bf16[1024,128]{1,0:T(8,128)(2,1)}, bf16[1024,128]{1,0:T(8,128)(2,1)S(1)}, u32[]{:S(2)}) copy-start(bf16[1024,128]{1,0:T(8,128)(2,1)S(1)} %all_gather.16) | copy-start | bytes 786436
  76.2 8.7 %collective-permute-start.6 = (bf16[1024,128]{1,0:T(8,128)(2,1)S(1)}, bf16[1024,128]{1,0:T(8,128)(2,1)}, u32[]{:S(2)}, u32[]{:S(2)}) collective-permute-start(bf16[1024,128]{1,0:T(8,128)(2,1)S(1)} %all_gather.16), channel_id=1, source_target_pairs={{0,4},{4,0},{8,12},{12,8},{16,20},{20,16},{24,28},{28,24},{1,5},{5... | collective-permute-start | bytes 786440 | tf_op jit(solution)/shard_map/ppermute | solution.py:16
  85.9 0.7 copy-start.1
  87.5 29.5 %copy-start.7 = (bf16[256,8192]{1,0:T(8,128)(2,1)S(1)}, bf16[256,8192]{1,0:T(8,128)(2,1)}, u32[]{:S(2)}) copy-start(bf16[256,8192]{1,0:T(8,128)(2,1)} %param.9) | copy-start | bytes 12582916
  87.5 46.8 %collective-permute-start.7 = (bf16[2048,128]{1,0:T(8,128)(2,1)}, bf16[2048,128]{1,0:T(8,128)(2,1)}, u32[]{:S(2)}, u32[]{:S(2)}) collective-permute-start(bf16[2048,128]{1,0:T(8,128)(2,1)} %pad_maximum_fusion.2), channel_id=1, source_target_pairs={{0,8},{8,0},{4,12},{12,4},{16,24},{24,16},{20,28},{28,20},{1,9},{9... | collective-permute-start | bytes 1572872 | tf_op jit(solution)/shard_map/ppermute | solution.py:16
  117.0 17.3 %copy-start.2 = (bf16[1024,128]{1,0:T(8,128)(2,1)S(1)}, bf16[1024,128]{1,0:T(8,128)(2,1)}, u32[]{:S(2)}) copy-start(bf16[1024,128]{1,0:T(8,128)(2,1)} %copy-done.1) | copy-start | bytes 786436
  119.2 18.3 %copy-start.4 = (bf16[256,128]{1,0:T(8,128)(2,1)S(1)}, bf16[256,128]{1,0:T(8,128)(2,1)}, u32[]{:S(2)}) copy-start(bf16[256,128]{1,0:T(8,128)(2,1)} %param.12) | copy-start | bytes 196612
  124.6 9.0 %collective-permute-start.8 = (bf16[32,128]{1,0:T(8,128)(2,1)S(1)}, bf16[32,128]{1,0:T(8,128)(2,1)S(1)}, u32[]{:S(2)}, u32[]{:S(2)}) collective-permute-start(bf16[32,128]{1,0:T(8,128)(2,1)S(1)} %all_gather.17), channel_id=1, source_target_pairs={{0,4},{4,0},{8,12},{12,8},{16,20},{20,16},{24,28},{28,24},{1,5},{5... | collective-permute-start | bytes 24584 | tf_op jit(solution)/shard_map/ppermute | solution.py:16
  132.5 14.3 %collective-permute-start.10 = (bf16[2048,128]{1,0:T(8,128)(2,1)S(1)}, bf16[2048,128]{1,0:T(8,128)(2,1)}, u32[]{:S(2)}, u32[]{:S(2)}) collective-permute-start(bf16[2048,128]{1,0:T(8,128)(2,1)S(1)} %all_gather.18), channel_id=1, source_target_pairs={{0,4},{4,0},{8,12},{12,8},{16,20},{20,16},{24,28},{28,24},{1,5},{5... | collective-permute-start | bytes 1572872 | tf_op jit(solution)/shard_map/ppermute | solution.py:16
  133.6 3.8 %collective-permute-start.9 = (bf16[64,128]{1,0:T(8,128)(2,1)S(1)}, bf16[64,128]{1,0:T(8,128)(2,1)S(1)}, u32[]{:S(2)}, u32[]{:S(2)}) collective-permute-start(bf16[64,128]{1,0:T(8,128)(2,1)S(1)} %pad_maximum_fusion.5), channel_id=1, source_target_pairs={{0,8},{8,0},{4,12},{12,4},{16,24},{24,16},{20,28},{28,20},{1,9},{9... | collective-permute-start | bytes 49160 | tf_op jit(solution)/shard_map/ppermute | solution.py:16
  138.5 9.4 %copy-start.5 = (bf16[512,64]{0,1:T(8,128)(2,1)S(1)}, bf16[512,64]{0,1:T(8,128)(2,1)}, u32[]{:S(2)}) copy-start(bf16[512,64]{0,1:T(8,128)(2,1)} %param.13) | copy-start | bytes 196612
  144.0 3.9 %collective-permute-start.11 = (bf16[32,128]{1,0:T(8,128)(2,1)S(1)}, bf16[32,128]{1,0:T(8,128)(2,1)S(1)}, u32[]{:S(2)}, u32[]{:S(2)}) collective-permute-start(bf16[32,128]{1,0:T(8,128)(2,1)S(1)} %all_gather.19), channel_id=1, source_target_pairs={{0,4},{4,0},{8,12},{12,8},{16,20},{20,16},{24,28},{28,24},{1,5},{5... | collective-permute-start | bytes 24584 | tf_op jit(solution)/shard_map/ppermute | solution.py:16
  148.1 3.8 %copy-start.6 = (f32[256,128]{0,1:T(8,128)S(1)}, f32[256,128]{0,1:T(8,128)}, u32[]{:S(2)}) copy-start(f32[256,128]{0,1:T(8,128)} %get-tuple-element.24) | copy-start | bytes 393220
where the time goes:
time: 154 us; the launch traced here: 153 us
  waiting for transfers between devices  61.5 us (40%)
  blocking collectives  49.8 us (32%)
  starting transfers between devices  15.8 us (10%)
  matrix products  9.76 us (6%)
  other arithmetic  9.43 us (6%)
  local copies, waits for them, and re-layouts  4.34 us (3%)
  between operations  2.28 us (1%)
    ppermute x12, waiting for transfers between devices, from_partner(): return lax.ppermute(block, axis, route)  61.5 us
    all_gather x5, blocking collectives, collect(): panel = lax.all_gather(piece, 'sep', axis=0, tiled=True)  29.1 us
    unnamed x2, blocking collectives  20.8 us
    ppermute x12, starting transfers between devices, from_partner(): return lax.ppermute(block, axis, route)  15.8 us
    dot_general x3, matrix products, apply_inverse(): return jnp.dot(inverse, panel, preferred_element_type=jnp.float32)  6.77 us
    select_n x9, other arithmetic, collect(): first = jnp.where(upper, partner, panel)  5.36 us
  transfers between devices with their start and end apart: 12, of which 8 were waited for; matrix products, arithmetic and copies ran while one was open for 8% of the time, Pallas kernels for 0%

commit v1 on v0

--- a/solution.py
+++ b/solution.py
@@ -2,6 +2,7 @@
 import jax.numpy as jnp
 from jax import lax
 from jax.sharding import PartitionSpec as P
+from jax.lax import axis_index, axis_size, ppermute
 
 BLOCK = 8
 
@@ -36,7 +37,23 @@
     lower_side = right_side[2 * dev_rows :]
 
     def collect(piece, depth_bits):
-        panel = lax.all_gather(piece, "sep", axis=0, tiled=True)
+        x_now, r_now, local_now = (axis_size("sep"), axis_index("sep"), piece.shape[0])
+        shelf = [(dev_j, (dev_j + 1) % x_now) for dev_j in range(x_now)]
+        pool = [(dev_j, (dev_j - 1) % x_now) for dev_j in range(x_now)]
+        panel = jnp.zeros((*piece.shape[:0], x_now * local_now, *piece.shape[1:]), piece.dtype)
+        arr_now = out_arr = piece
+        panel = lax.dynamic_update_slice_in_dim(panel, piece, r_now * local_now, axis=0)
+        field_out = x_now // 2
+        for i0 in tuple(range(1, field_out + 1)):
+            arr_now = ppermute(arr_now, "sep", shelf)
+            panel = lax.dynamic_update_slice_in_dim(
+                panel, arr_now, (r_now - i0) % x_now * local_now, axis=0
+            )
+            if i0 < x_now - field_out:
+                out_arr = ppermute(out_arr, "sep", pool)
+                panel = lax.dynamic_update_slice_in_dim(
+                    panel, out_arr, (r_now + i0) % x_now * local_now, axis=0
+                )
         for bit_index in range(depth_bits):
             partner = from_partner(panel, "leaf", bit_index)
             upper = leaf_index >> bit_index & 1 == 1

time: 154 us -> 147 us (0.955)
  blocking collectives: 49.8 us -> 20.8 us
  waiting for transfers between devices: 61.5 us -> 75.6 us
  starting transfers between devices: 15.8 us -> 23.4 us
  local copies, waits for them, and re-layouts: 4.34 us -> 10.2 us
  other arithmetic: 9.43 us -> 6.52 us
  matrix products: 9.76 us -> 7.93 us
    all_gather x5 -> x0, blocking collectives: 29.1 us -> none  [collect(): panel = lax.all_gather(piece, 'sep', axis=0, tiled=True)]
    ppermute x0 -> x15, waiting for transfers between devices: none -> 20.9 us  [the longest x10 18.1 us: collect(): arr_now = ppermute(arr_now, 'sep', shelf)]
    ppermute x0 -> x15, starting transfers between devices: none -> 7.31 us  [the longest x5 5.64 us: collect(): out_arr = ppermute(out_arr, 'sep', pool)]
    ppermute x12, waiting for transfers between devices: 61.5 us -> 54.7 us  [from_partner(): return lax.ppermute(block, axis, route)]
    dynamic_update_slice x0 -> x16, local copies, waits for them, and re-layouts: none -> 6.56 us  [the longest x10 3.21 us: collect(): lax.dynamic_update_slice_in_dim(panel, arr_now, (r_now - i0) % x_now * lo...]
    convert_element_type x4 -> x0, other arithmetic: 1.86 us -> none  [the longest x1 0.92 us: on_device(): middle_words = (middle_side - lower_accum[dev_rows:]).astype(jnp.bfloat16)]
  transfers between devices with their start and end apart: 12 -> 27, of which waited for: 8 -> 18; matrix products, arithmetic and copies ran while one was open for 8% -> 10% of each run, Pallas kernels for 0% -> 0%
where the time goes in v1:
time: 147 us
  waiting for transfers between devices  75.6 us (51%)
  starting transfers between devices  23.4 us (16%)
  blocking collectives  20.8 us (14%)
  local copies, waits for them, and re-layouts  10.2 us (7%)
  matrix products  7.93 us (5%)
  other arithmetic  6.52 us (4%)
  between operations  2.4 us (2%)
    ppermute x12, waiting for transfers between devices, from_partner(): return lax.ppermute(block, axis, route)  54.7 us
    unnamed x2, blocking collectives  20.8 us
    ppermute x10, waiting for transfers between devices, collect(): arr_now = ppermute(arr_now, 'sep', shelf)  18.1 us
    ppermute x12, starting transfers between devices, from_partner(): return lax.ppermute(block, axis, route)  16.1 us
    dot_general x3, matrix products, apply_inverse(): return jnp.dot(inverse, panel, preferred_element_type=jnp.float32)  6.08 us
    ppermute x5, starting transfers between devices, collect(): out_arr = ppermute(out_arr, 'sep', pool)  5.64 us
    select_n x9, other arithmetic, collect(): first = jnp.where(upper, partner, panel)  5 us
    dynamic_update_slice x10, local copies, waits for them, and re-layouts, collect(): lax.dynamic_update_slice_in_dim(panel, arr_now, (r_now - i0) % x_now * lo...  3.21 us
  transfers between devices with their start and end apart: 27, of which 18 were waited for; matrix products, arithmetic and copies ran while one was open for 10% of the time, Pallas kernels for 0%

profile of v1, /device:TPU:0, one launch (start us, length us, event | category | flops | bytes accessed | tf_op | source)
XLA Modules:
  0.0 146.9 jit_solution(2363742735692463139)
XLA Ops:
  0.0 0.9 broadcast_in_dim.2
  0.9 1.7 %constant_dynamic-update-slice_fusion.7 = (bf16[2048,128]{1,0:T(8,128)(2,1)}, bf16[512,128]{1,0:T(8,128)(2,1)S(1)}) fusion(bf16[2048,128]{1,0:T(8,128)(2,1)} %broadcast_in_dim.2, s32[]{:T(128)S(6)} %select_n.242, f32[1024,128]{1,0:T(8,128)} %param.8), kind=kLoop, calls=%fused_computation.72 | loop fusion | bytes 393220 | tf_op jit(solution)/shard_map/dynamic_update_slice | solution.py:45
  2.6 1.0 fusion.44
  3.6 3.0 %collective-permute-start = (f32[32,128]{1,0:T(8,128)S(1)}, f32[32,128]{1,0:T(8,128)S(1)}, u32[]{:S(2)}, u32[]{:S(2)}) collective-permute-start(f32[32,128]{1,0:T(8,128)S(1)} %slice_select_fusion.2), channel_id=1, source_target_pairs={{0,4},{4,0},{8,12},{12,8},{16,20},{20,16},{24,28},{28,24},{1,5},{5... | collective-permute-start | bytes 49160 | tf_op jit(solution)/shard_map/ppermute | solution.py:17
  7.3 1.3 dynamic-slice
  9.2 10.7 %all-reduce = f32[32,128]{1,0:T(8,128)S(1)} all-reduce(f32[32,128]{1,0:T(8,128)S(1)} %select_add_fusion.2), channel_id=2, replica_groups=mesh['leaf'=8,'sep'=4] {'sep'}, use_global_device_ids=true, to_apply=%region_0.1.clone | all-reduce | flops 4096 | bytes 32768
  20.4 1.6 %collective-permute-start.1 = (f32[64,128]{1,0:T(8,128)S(1)}, f32[64,128]{1,0:T(8,128)S(1)}, u32[]{:S(2)}, u32[]{:S(2)}) collective-permute-start(f32[64,128]{1,0:T(8,128)S(1)} %slice_select_fusion), channel_id=1, source_target_pairs={{0,8},{8,0},{4,12},{12,4},{16,24},{24,16},{20,28},{28,20},{1,9},{9... | collective-permute-start | bytes 98312 | tf_op jit(solution)/shard_map/ppermute | solution.py:17
  22.7 1.7 %collective-permute-done.1 = f32[64,128]{1,0:T(8,128)S(1)} collective-permute-done((f32[64,128]{1,0:T(8,128)S(1)}, f32[64,128]{1,0:T(8,128)S(1)}, u32[]{:S(2)}, u32[]{:S(2)}) %collective-permute-start.1) | collective-permute-done | bytes 32800 | tf_op jit(solution)/shard_map/ppermute | solution.py:17
  24.4 0.6 collective-permute-start.2
  25.0 3.2 %collective-permute-done.2 = f32[32,128]{1,0:T(8,128)S(1)} collective-permute-done((f32[32,128]{1,0:T(8,128)S(1)}, f32[32,128]{1,0:T(8,128)S(1)}, u32[]{:S(2)}, u32[]{:S(2)}) %collective-permute-start.2) | collective-permute-done | bytes 16416 | tf_op jit(solution)/shard_map/ppermute | solution.py:17
  28.2 10.1 %all-reduce.1 = f32[32,128]{1,0:T(8,128)S(1)} all-reduce(f32[32,128]{1,0:T(8,128)S(1)} %select_add_fusion.1), channel_id=3, replica_groups=mesh['leaf'=8,'sep'=4] {'sep'}, use_global_device_ids=true, to_apply=%region_1.2.clone | all-reduce | flops 4096 | bytes 32768
  38.7 1.7 %collective-permute-start.4 = (bf16[256,128]{1,0:T(8,128)(2,1)S(1)}, bf16[256,128]{1,0:T(8,128)(2,1)S(1)}, u32[]{:S(2)}, u32[]{:S(2)}) collective-permute-start(bf16[256,128]{1,0:T(8,128)(2,1)S(1)} %get-tuple-element.14), channel_id=1, source_target_pairs={{0,3},{1,0},{2,1},{3,2},{4,7},{5,4},{6,5},{7,6},{8,11},{9,8},{10,9... | collective-permute-start | bytes 196616 | tf_op jit(solution)/shard_map/ppermute | solution.py:53
  40.3 1.9 %collective-permute-done.3 = bf16[256,128]{1,0:T(8,128)(2,1)S(1)} collective-permute-done((bf16[256,128]{1,0:T(8,128)(2,1)S(1)}, bf16[256,128]{1,0:T(8,128)(2,1)S(1)}, u32[]{:S(2)}, u32[]{:S(2)}) %collective-permute-start.3) | collective-permute-done | bytes 65568 | tf_op jit(solution)/shard_map/ppermute | solution.py:48
  42.3 3.6 %collective-permute-done.5 = bf16[256,128]{1,0:T(8,128)(2,1)S(1)} collective-permute-done((bf16[256,128]{1,0:T(8,128)(2,1)S(1)}, bf16[256,128]{1,0:T(8,128)(2,1)S(1)}, u32[]{:S(2)}, u32[]{:S(2)}) %collective-permute-start.5) | collective-permute-done | bytes 65568 | tf_op jit(solution)/shard_map/ppermute | solution.py:48
  46.0 0.6 collective-permute-start.6
  46.6 6.5 %collective-permute-done.6 = bf16[1024,128]{1,0:T(8,128)(2,1)S(1)} collective-permute-done((bf16[1024,128]{1,0:T(8,128)(2,1)S(1)}, bf16[1024,128]{1,0:T(8,128)(2,1)S(1)}, u32[]{:S(2)}, u32[]{:S(2)}) %collective-permute-start.6) | collective-permute-done | bytes 262176 | tf_op jit(solution)/shard_map/ppermute | solution.py:17
  53.2 1.6 %collective-permute-start.7 = (bf16[2048,128]{1,0:T(8,128)(2,1)S(1)}, bf16[2048,128]{1,0:T(8,128)(2,1)S(1)}, u32[]{:S(2)}, u32[]{:S(2)}) collective-permute-start(bf16[2048,128]{1,0:T(8,128)(2,1)S(1)} %pad_maximum_fusion.1), channel_id=1, source_target_pairs={{0,8},{8,0},{4,12},{12,4},{16,24},{24,16},{20,28},{28,20},{1,9},{9... | collective-permute-start | bytes 1572872 | tf_op jit(solution)/shard_map/ppermute | solution.py:17
  54.8 10.1 %collective-permute-done.7 = bf16[2048,128]{1,0:T(8,128)(2,1)S(1)} collective-permute-done((bf16[2048,128]{1,0:T(8,128)(2,1)S(1)}, bf16[2048,128]{1,0:T(8,128)(2,1)S(1)}, u32[]{:S(2)}, u32[]{:S(2)}) %collective-permute-start.7) | collective-permute-done | bytes 524320 | tf_op jit(solution)/shard_map/ppermute | solution.py:17
  65.2 1.1 pad_maximum_fusion
  66.3 2.6 %collective-permute-start.8 = (bf16[4096,128]{1,0:T(8,128)(2,1)}, bf16[4096,128]{1,0:T(8,128)(2,1)}, u32[]{:S(2)}, u32[]{:S(2)}) collective-permute-start(bf16[4096,128]{1,0:T(8,128)(2,1)} %pad_maximum_fusion), channel_id=1, source_target_pairs={{0,16},{16,0},{4,20},{20,4},{8,24},{24,8},{12,28},{28,12},{1,17},{... | collective-permute-start | bytes 3145736 | tf_op jit(solution)/shard_map/ppermute | solution.py:17
  68.8 1.0 collective-permute-start.19
  69.8 0.8 collective-permute-start.10
  70.6 1.9 %collective-permute-done.9 = bf16[256,128]{1,0:T(8,128)(2,1)S(1)} collective-permute-done((bf16[256,128]{1,0:T(8,128)(2,1)S(1)}, bf16[256,128]{1,0:T(8,128)(2,1)S(1)}, u32[]{:S(2)}, u32[]{:S(2)}) %collective-permute-start.9) | collective-permute-done | bytes 65568 | tf_op jit(solution)/shard_map/ppermute | solution.py:48
  73.0 3.2 %collective-permute-done.11 = bf16[256,128]{1,0:T(8,128)(2,1)S(1)} collective-permute-done((bf16[256,128]{1,0:T(8,128)(2,1)S(1)}, bf16[256,128]{1,0:T(8,128)(2,1)S(1)}, u32[]{:S(2)}, u32[]{:S(2)}) %collective-permute-start.11) | collective-permute-done | bytes 65568 | tf_op jit(solution)/shard_map/ppermute | solution.py:48
  76.3 1.8 %collective-permute-start.12 = (bf16[1024,128]{1,0:T(8,128)(2,1)S(1)}, bf16[1024,128]{1,0:T(8,128)(2,1)}, u32[]{:S(2)}, u32[]{:S(2)}) collective-permute-start(bf16[1024,128]{1,0:T(8,128)(2,1)S(1)} %constant_dynamic-update-slice_fusion.12), channel_id=1, source_target_pairs={{0,4},{4,0},{8,12},{12,8},{16,20},{20,16},{24,28},{28,24},{1,5},{5... | collective-permute-start | bytes 786440 | tf_op jit(solution)/shard_map/ppermute | solution.py:17
  78.5 1.6 %constant_dynamic-update-slice_fusion.6 = bf16[2048,128]{1,0:T(8,128)(2,1)} fusion(bf16[2048,128]{1,0:T(8,128)(2,1)} %get-tuple-element.5, bf16[512,128]{1,0:T(8,128)(2,1)} %collective-permute-done.19, s32[]{:T(128)S(6)} %select_n.243), kind=kLoop, calls=%fused_computation.71 | loop fusion | bytes 262148 | tf_op jit(solution)/shard_map/dynamic_update_slice | solution.py:49
  80.1 1.8 %collective-permute-done.20 = bf16[512,128]{1,0:T(8,128)(2,1)} collective-permute-done((bf16[512,128]{1,0:T(8,128)(2,1)S(1)}, bf16[512,128]{1,0:T(8,128)(2,1)}, u32[]{:S(2)}, u32[]{:S(2)}) %collective-permute-start.20) | collective-permute-done | bytes 131104 | tf_op jit(solution)/shard_map/ppermute | solution.py:53
  81.9 1.6 %constant_dynamic-update-slice_fusion.5 = bf16[2048,128]{1,0:T(8,128)(2,1)} fusion(bf16[2048,128]{1,0:T(8,128)(2,1)} %constant_dynamic-update-slice_fusion.6, bf16[512,128]{1,0:T(8,128)(2,1)} %collective-permute-done.20, s32[]{:T(128)S(6)} %select_n.244), kind=kLoop, calls=%fused_computation.70 | loop fusion | bytes 262148 | tf_op jit(solution)/shard_map/dynamic_update_slice | solution.py:54
  83.4 1.8 %broadcast_select_fusion.9 = (bf16[1024,128]{1,0:T(8,128)(2,1)S(1)}, bf16[1024,128]{1,0:T(8,128)(2,1)}) fusion(bf16[1024,128]{1,0:T(8,128)(2,1)} %collective-permute-done.12, bf16[1024,128]{1,0:T(8,128)(2,1)} %copy-done.2, pred[]{:T(512)S(6)} %eq.112), kind=kLoop, calls=%fused_computation.30 | loop fusion | flops 262144 | bytes 1048577 | tf_op jit(solution)/shard_map/jit(_where)/select_n | solution.py:60
  85.2 26.8 %collective-permute-done.8 = bf16[4096,128]{1,0:T(8,128)(2,1)} collective-permute-done((bf16[4096,128]{1,0:T(8,128)(2,1)}, bf16[4096,128]{1,0:T(8,128)(2,1)}, u32[]{:S(2)}, u32[]{:S(2)}) %collective-permute-start.8) | collective-permute-done | bytes 1048608 | tf_op jit(solution)/shard_map/ppermute | solution.py:17
  112.0 1.6 %broadcast_select_fusion.1 = (bf16[4096,128]{1,0:T(8,128)(2,1)S(1)}, bf16[4096,128]{1,0:T(8,128)(2,1)S(1)}) fusion(bf16[4096,128]{1,0:T(8,128)(2,1)} %collective-permute-done.8, pred[]{:T(512)S(6)} %eq.110, bf16[2048,128]{1,0:T(8,128)(2,1)S(1)} %get-tuple-element.22, bf16[2048,128]{1,0:T(8,128)(2,1)S(1)} %get-tuple-element.21), kind=kLoop, calls=%fused_computation.18 | loop fusion | flops 3145728 | bytes 4194305 | tf_op jit(solution)/shard_map/jit(_where)/select_n | solution.py:60
  113.6 1.5 %fusion.42 = (bf16[256,128]{0,1:T(8,128)(2,1)S(1)}, f32[256,128]{0,1:T(8,128)S(1)}) fusion(bf16[256,8192]{1,0:T(8,128)(2,1)S(1)} %copy-done.9, bf16[4096,128]{1,0:T(8,128)(2,1)S(1)} %get-tuple-element.16, bf16[4096,128]{1,0:T(8,128)(2,1)S(1)} %get-tuple-element.15), kind=kOutput, calls=%fused_computation.102 | convolution fusion | flops 541097984 | bytes 6488064 | tf_op jit(solution)/shard_map/dot_general | solution.py:67
  115.6 0.7 collective-permute-start.13
  116.3 1.4 collective-permute-start.15
  117.8 0.8 collective-permute-done.14
  119.1 2.5 %collective-permute-done.16 = bf16[8,128]{1,0:T(8,128)(2,1)S(1)} collective-permute-done((bf16[8,128]{1,0:T(8,128)(2,1)S(1)}, bf16[8,128]{1,0:T(8,128)(2,1)S(1)}, u32[]{:S(2)}, u32[]{:S(2)}) %collective-permute-start.16) | collective-permute-done | bytes 2080 | tf_op jit(solution)/shard_map/ppermute | solution.py:48
  121.5 2.2 %collective-permute-start.17 = (bf16[32,128]{1,0:T(8,128)(2,1)S(1)}, bf16[32,128]{1,0:T(8,128)(2,1)S(1)}, u32[]{:S(2)}, u32[]{:S(2)}) collective-permute-start(bf16[32,128]{1,0:T(8,128)(2,1)S(1)} %constant_dynamic-update-slice_fusion.8), channel_id=1, source_target_pairs={{0,4},{4,0},{8,12},{12,8},{16,20},{20,16},{24,28},{28,24},{1,5},{5... | collective-permute-start | bytes 24584 | tf_op jit(solution)/shard_map/ppermute | solution.py:17
  123.7 1.6 %constant_dynamic-update-slice_fusion.4 = bf16[2048,128]{1,0:T(8,128)(2,1)} fusion(bf16[2048,128]{1,0:T(8,128)(2,1)} %constant_dynamic-update-slice_fusion.5, bf16[512,128]{1,0:T(8,128)(2,1)} %collective-permute-done.21, s32[]{:T(128)S(6)} %select_n.245), kind=kLoop, calls=%fused_computation.69 | loop fusion | bytes 262148 | tf_op jit(solution)/shard_map/dynamic_update_slice | solution.py:49
  125.4 0.7 collective-permute-start.18
  126.1 4.3 %collective-permute-done.13 = bf16[2048,128]{1,0:T(8,128)(2,1)S(1)} collective-permute-done((bf16[2048,128]{1,0:T(8,128)(2,1)S(1)}, bf16[2048,128]{1,0:T(8,128)(2,1)S(1)}, u32[]{:S(2)}, u32[]{:S(2)}) %collective-permute-start.13) | collective-permute-done | bytes 524320 | tf_op jit(solution)/shard_map/ppermute | solution.py:17
  130.9 0.9 fusion.43
  132.2 1.7 %collective-permute-start.24 = (bf16[8,128]{1,0:T(8,128)(2,1)S(1)}, bf16[8,128]{1,0:T(8,128)(2,1)S(1)}, u32[]{:S(2)}, u32[]{:S(2)}) collective-permute-start(bf16[8,128]{1,0:T(8,128)(2,1)S(1)} %get-tuple-element.8), channel_id=1, source_target_pairs={{0,3},{1,0},{2,1},{3,2},{4,7},{5,4},{6,5},{7,6},{8,11},{9,8},{10,9... | collective-permute-start | bytes 6152 | tf_op jit(solution)/shard_map/ppermute | solution.py:53
  133.9 1.3 collective-permute-done.23
  135.3 3.0 %collective-permute-done.25 = bf16[8,128]{1,0:T(8,128)(2,1)S(1)} collective-permute-done((bf16[8,128]{1,0:T(8,128)(2,1)S(1)}, bf16[8,128]{1,0:T(8,128)(2,1)S(1)}, u32[]{:S(2)}, u32[]{:S(2)}) %collective-permute-start.25) | collective-permute-done | bytes 2080 | tf_op jit(solution)/shard_map/ppermute | solution.py:48
  138.8 1.1 broadcast_select_fusion.3
  139.9 2.0 %collective-permute-done.26 = bf16[32,128]{1,0:T(8,128)(2,1)S(1)} collective-permute-done((bf16[32,128]{1,0:T(8,128)(2,1)S(1)}, bf16[32,128]{1,0:T(8,128)(2,1)S(1)}, u32[]{:S(2)}, u32[]{:S(2)}) %collective-permute-start.26) | collective-permute-done | bytes 8224 | tf_op jit(solution)/shard_map/ppermute | solution.py:17
  142.1 3.7 %fusion.4 = f32[512,128]{0,1:T(8,128)S(1)} fusion(f32[128,512]{1,0:T(8,128)S(1)} %fusion.25, bf16[512,4096]{1,0:T(8,128)(2,1)} %param.11, bf16[2048,128]{1,0:T(8,128)(2,1)S(1)} %get-tuple-element.18, bf16[2048,128]{1,0:T(8,128)(2,1)S(1)} %get-tuple-element.17), kind=kOutput, calls=%fused_computation.5 | convolution fusion | flops 539033600 | bytes 5767168 | tf_op jit(solution)/shard_map/dot_general | solution.py:67
  145.9 1.0 copy.15
  (98 shorter events, 4.9 us)
Async XLA Ops:
  0.0 130.9 %copy-start = (bf16[256,4096]{1,0:T(8,128)(2,1)S(1)}, bf16[256,4096]{1,0:T(8,128)(2,1)}, u32[]{:S(2)}) copy-start(bf16[256,4096]{1,0:T(8,128)(2,1)} %param.10) | copy-start | bytes 6291460
  0.0 20.1 %copy-start.3 = (f32[1024,128]{1,0:T(8,128)S(1)}, f32[1024,128]{1,0:T(8,128)}, u32[]{:S(2)}) copy-start(f32[1024,128]{1,0:T(8,128)} %param.8) | copy-start | bytes 1572868
  0.0 20.2 %copy-start.4 = (bf16[256,128]{1,0:T(8,128)(2,1)S(1)}, bf16[256,128]{1,0:T(8,128)(2,1)}, u32[]{:S(2)}) copy-start(bf16[256,128]{1,0:T(8,128)(2,1)} %param.12) | copy-start | bytes 196612
  3.6 5.6 %collective-permute-start = (f32[32,128]{1,0:T(8,128)S(1)}, f32[32,128]{1,0:T(8,128)S(1)}, u32[]{:S(2)}, u32[]{:S(2)}) collective-permute-start(f32[32,128]{1,0:T(8,128)S(1)} %slice_select_fusion.2), channel_id=1, source_target_pairs={{0,4},{4,0},{8,12},{12,8},{16,20},{20,16},{24,28},{28,24},{1,5},{5... | collective-permute-start | bytes 49160 | tf_op jit(solution)/shard_map/ppermute | solution.py:17
  20.2 4.2 %copy-start.7 = (bf16[256,128]{1,0:T(8,128)(2,1)}, bf16[256,128]{1,0:T(8,128)(2,1)S(1)}, u32[]{:S(2)}) copy-start(bf16[256,128]{1,0:T(8,128)(2,1)S(1)} %get-tuple-element.10) | copy-start | bytes 196612
  20.4 4.0 %collective-permute-start.1 = (f32[64,128]{1,0:T(8,128)S(1)}, f32[64,128]{1,0:T(8,128)S(1)}, u32[]{:S(2)}, u32[]{:S(2)}) collective-permute-start(f32[64,128]{1,0:T(8,128)S(1)} %slice_select_fusion), channel_id=1, source_target_pairs={{0,8},{8,0},{4,12},{12,4},{16,24},{24,16},{20,28},{28,20},{1,9},{9... | collective-permute-start | bytes 98312 | tf_op jit(solution)/shard_map/ppermute | solution.py:17
  24.4 3.8 %collective-permute-start.2 = (f32[32,128]{1,0:T(8,128)S(1)}, f32[32,128]{1,0:T(8,128)S(1)}, u32[]{:S(2)}, u32[]{:S(2)}) collective-permute-start(f32[32,128]{1,0:T(8,128)S(1)} %slice_select_fusion.1), channel_id=1, source_target_pairs={{0,4},{4,0},{8,12},{12,8},{16,20},{20,16},{24,28},{28,24},{1,5},{5... | collective-permute-start | bytes 49160 | tf_op jit(solution)/shard_map/ppermute | solution.py:17
  38.5 3.7 %collective-permute-start.3 = (bf16[256,128]{1,0:T(8,128)(2,1)S(1)}, bf16[256,128]{1,0:T(8,128)(2,1)S(1)}, u32[]{:S(2)}, u32[]{:S(2)}) collective-permute-start(bf16[256,128]{1,0:T(8,128)(2,1)S(1)} %get-tuple-element.14), channel_id=1, source_target_pairs={{0,1},{1,2},{2,3},{3,0},{4,5},{5,6},{6,7},{7,4},{8,9},{9,10},{10,1... | collective-permute-start | bytes 196616 | tf_op jit(solution)/shard_map/ppermute | solution.py:48
  38.7 3.6 %collective-permute-start.4 = (bf16[256,128]{1,0:T(8,128)(2,1)S(1)}, bf16[256,128]{1,0:T(8,128)(2,1)S(1)}, u32[]{:S(2)}, u32[]{:S(2)}) collective-permute-start(bf16[256,128]{1,0:T(8,128)(2,1)S(1)} %get-tuple-element.14), channel_id=1, source_target_pairs={{0,3},{1,0},{2,1},{3,2},{4,7},{5,4},{6,5},{7,6},{8,11},{9,8},{10,9... | collective-permute-start | bytes 196616 | tf_op jit(solution)/shard_map/ppermute | solution.py:53
  42.3 3.7 %collective-permute-start.5 = (bf16[256,128]{1,0:T(8,128)(2,1)S(1)}, bf16[256,128]{1,0:T(8,128)(2,1)S(1)}, u32[]{:S(2)}, u32[]{:S(2)}) collective-permute-start(bf16[256,128]{1,0:T(8,128)(2,1)S(1)} %collective-permute-done.3), channel_id=1, source_target_pairs={{0,1},{1,2},{2,3},{3,0},{4,5},{5,6},{6,7},{7,4},{8,9},{9,10},{10,1... | collective-permute-start | bytes 196616 | tf_op jit(solution)/shard_map/ppermute | solution.py:48
  46.0 7.1 %collective-permute-start.6 = (bf16[1024,128]{1,0:T(8,128)(2,1)S(1)}, bf16[1024,128]{1,0:T(8,128)(2,1)S(1)}, u32[]{:S(2)}, u32[]{:S(2)}) collective-permute-start(bf16[1024,128]{1,0:T(8,128)(2,1)S(1)} %constant_dynamic-update-slice_fusion.16), channel_id=1, source_target_pairs={{0,4},{4,0},{8,12},{12,8},{16,20},{20,16},{24,28},{28,24},{1,5},{5... | collective-permute-start | bytes 786440 | tf_op jit(solution)/shard_map/ppermute | solution.py:17
  53.2 15.7 %copy-start.8 = (bf16[256,128]{1,0:T(8,128)(2,1)S(1)}, bf16[256,128]{1,0:T(8,128)(2,1)}, u32[]{:S(2)}) copy-start(bf16[256,128]{1,0:T(8,128)(2,1)} %copy-done.7) | copy-start | bytes 196612
  53.2 11.8 %collective-permute-start.7 = (bf16[2048,128]{1,0:T(8,128)(2,1)S(1)}, bf16[2048,128]{1,0:T(8,128)(2,1)S(1)}, u32[]{:S(2)}, u32[]{:S(2)}) collective-permute-start(bf16[2048,128]{1,0:T(8,128)(2,1)S(1)} %pad_maximum_fusion.1), channel_id=1, source_target_pairs={{0,8},{8,0},{4,12},{12,4},{16,24},{24,16},{20,28},{28,20},{1,9},{9... | collective-permute-start | bytes 1572872 | tf_op jit(solution)/shard_map/ppermute | solution.py:17
  66.3 45.7 %collective-permute-start.8 = (bf16[4096,128]{1,0:T(8,128)(2,1)}, bf16[4096,128]{1,0:T(8,128)(2,1)}, u32[]{:S(2)}, u32[]{:S(2)}) collective-permute-start(bf16[4096,128]{1,0:T(8,128)(2,1)} %pad_maximum_fusion), channel_id=1, source_target_pairs={{0,16},{16,0},{4,20},{20,4},{8,24},{24,8},{12,28},{28,12},{1,17},{... | collective-permute-start | bytes 3145736 | tf_op jit(solution)/shard_map/ppermute | solution.py:17
  68.8 3.7 %collective-permute-start.9 = (bf16[256,128]{1,0:T(8,128)(2,1)S(1)}, bf16[256,128]{1,0:T(8,128)(2,1)S(1)}, u32[]{:S(2)}, u32[]{:S(2)}) collective-permute-start(bf16[256,128]{1,0:T(8,128)(2,1)S(1)} %copy-done.8), channel_id=1, source_target_pairs={{0,1},{1,2},{2,3},{3,0},{4,5},{5,6},{6,7},{7,4},{8,9},{9,10},{10,1... | collective-permute-start | bytes 196616 | tf_op jit(solution)/shard_map/ppermute | solution.py:48
  68.8 9.2 %collective-permute-start.19 = (bf16[512,128]{1,0:T(8,128)(2,1)S(1)}, bf16[512,128]{1,0:T(8,128)(2,1)}, u32[]{:S(2)}, u32[]{:S(2)}) collective-permute-start(bf16[512,128]{1,0:T(8,128)(2,1)S(1)} %get-tuple-element.6), channel_id=1, source_target_pairs={{0,1},{1,2},{2,3},{3,0},{4,5},{5,6},{6,7},{7,4},{8,9},{9,10},{10,1... | collective-permute-start | bytes 393224 | tf_op jit(solution)/shard_map/ppermute | solution.py:48
  69.8 3.2 %collective-permute-start.10 = (bf16[256,128]{1,0:T(8,128)(2,1)S(1)}, bf16[256,128]{1,0:T(8,128)(2,1)S(1)}, u32[]{:S(2)}, u32[]{:S(2)}) collective-permute-start(bf16[256,128]{1,0:T(8,128)(2,1)S(1)} %copy-done.8), channel_id=1, source_target_pairs={{0,3},{1,0},{2,1},{3,2},{4,7},{5,4},{6,5},{7,6},{8,11},{9,8},{10,9... | collective-permute-start | bytes 196616 | tf_op jit(solution)/shard_map/ppermute | solution.py:53
  72.5 3.7 %collective-permute-start.11 = (bf16[256,128]{1,0:T(8,128)(2,1)S(1)}, bf16[256,128]{1,0:T(8,128)(2,1)S(1)}, u32[]{:S(2)}, u32[]{:S(2)}) collective-permute-start(bf16[256,128]{1,0:T(8,128)(2,1)S(1)} %collective-permute-done.9), channel_id=1, source_target_pairs={{0,1},{1,2},{2,3},{3,0},{4,5},{5,6},{6,7},{7,4},{8,9},{9,10},{10,1... | collective-permute-start | bytes 196616 | tf_op jit(solution)/shard_map/ppermute | solution.py:48
  76.2 7.2 %copy-start.2 = (bf16[1024,128]{1,0:T(8,128)(2,1)}, bf16[1024,128]{1,0:T(8,128)(2,1)S(1)}, u32[]{:S(2)}) copy-start(bf16[1024,128]{1,0:T(8,128)(2,1)S(1)} %constant_dynamic-update-slice_fusion.12) | copy-start | bytes 786436
  76.3 7.2 %collective-permute-start.12 = (bf16[1024,128]{1,0:T(8,128)(2,1)S(1)}, bf16[1024,128]{1,0:T(8,128)(2,1)}, u32[]{:S(2)}, u32[]{:S(2)}) collective-permute-start(bf16[1024,128]{1,0:T(8,128)(2,1)S(1)} %constant_dynamic-update-slice_fusion.12), channel_id=1, source_target_pairs={{0,4},{4,0},{8,12},{12,8},{16,20},{20,16},{24,28},{28,24},{1,5},{5... | collective-permute-start | bytes 786440 | tf_op jit(solution)/shard_map/ppermute | solution.py:17
  78.0 3.9 %collective-permute-start.20 = (bf16[512,128]{1,0:T(8,128)(2,1)S(1)}, bf16[512,128]{1,0:T(8,128)(2,1)}, u32[]{:S(2)}, u32[]{:S(2)}) collective-permute-start(bf16[512,128]{1,0:T(8,128)(2,1)S(1)} %get-tuple-element.6), channel_id=1, source_target_pairs={{0,3},{1,0},{2,1},{3,2},{4,7},{5,4},{6,5},{7,6},{8,11},{9,8},{10,9... | collective-permute-start | bytes 393224 | tf_op jit(solution)/shard_map/ppermute | solution.py:53
  78.0 45.7 %collective-permute-start.21 = (bf16[512,128]{1,0:T(8,128)(2,1)}, bf16[512,128]{1,0:T(8,128)(2,1)}, u32[]{:S(2)}, u32[]{:S(2)}) collective-permute-start(bf16[512,128]{1,0:T(8,128)(2,1)} %collective-permute-done.19), channel_id=1, source_target_pairs={{0,1},{1,2},{2,3},{3,0},{4,5},{5,6},{6,7},{7,4},{8,9},{9,10},{10,1... | collective-permute-start | bytes 393224 | tf_op jit(solution)/shard_map/ppermute | solution.py:48
  85.2 28.4 %copy-start.9 = (bf16[256,8192]{1,0:T(8,128)(2,1)S(1)}, bf16[256,8192]{1,0:T(8,128)(2,1)}, u32[]{:S(2)}) copy-start(bf16[256,8192]{1,0:T(8,128)(2,1)} %param.9) | copy-start | bytes 12582916
  113.6 1.9 %copy-start.1 = (bf16[1024,128]{1,0:T(8,128)(2,1)S(1)}, bf16[1024,128]{1,0:T(8,128)(2,1)}, u32[]{:S(2)}) copy-start(bf16[1024,128]{1,0:T(8,128)(2,1)} %get-tuple-element.24) | copy-start | bytes 786436
  115.1 15.6 %copy-start.5 = (bf16[256,128]{1,0:T(8,128)(2,1)S(1)}, bf16[256,128]{1,0:T(8,128)(2,1)}, u32[]{:S(2)}) copy-start(bf16[256,128]{1,0:T(8,128)(2,1)} %param.12) | copy-start | bytes 196612
  115.5 3.1 %collective-permute-start.14 = (bf16[8,128]{1,0:T(8,128)(2,1)S(1)}, bf16[8,128]{1,0:T(8,128)(2,1)S(1)}, u32[]{:S(2)}, u32[]{:S(2)}) collective-permute-start(bf16[8,128]{1,0:T(8,128)(2,1)S(1)} %get-tuple-element.12), channel_id=1, source_target_pairs={{0,1},{1,2},{2,3},{3,0},{4,5},{5,6},{6,7},{7,4},{8,9},{9,10},{10,1... | collective-permute-start | bytes 6152 | tf_op jit(solution)/shard_map/ppermute | solution.py:48
  115.6 14.9 %collective-permute-start.13 = (bf16[2048,128]{1,0:T(8,128)(2,1)S(1)}, bf16[2048,128]{1,0:T(8,128)(2,1)S(1)}, u32[]{:S(2)}, u32[]{:S(2)}) collective-permute-start(bf16[2048,128]{1,0:T(8,128)(2,1)S(1)} %pad_maximum_fusion.2), channel_id=1, source_target_pairs={{0,8},{8,0},{4,12},{12,4},{16,24},{24,16},{20,28},{28,20},{1,9},{9... | collective-permute-start | bytes 1572872 | tf_op jit(solution)/shard_map/ppermute | solution.py:17
  116.3 2.7 %collective-permute-start.15 = (bf16[8,128]{1,0:T(8,128)(2,1)S(1)}, bf16[8,128]{1,0:T(8,128)(2,1)S(1)}, u32[]{:S(2)}, u32[]{:S(2)}) collective-permute-start(bf16[8,128]{1,0:T(8,128)(2,1)S(1)} %get-tuple-element.12), channel_id=1, source_target_pairs={{0,3},{1,0},{2,1},{3,2},{4,7},{5,4},{6,5},{7,6},{8,11},{9,8},{10,9... | collective-permute-start | bytes 6152 | tf_op jit(solution)/shard_map/ppermute | solution.py:53
  118.5 3.0 %collective-permute-start.16 = (bf16[8,128]{1,0:T(8,128)(2,1)S(1)}, bf16[8,128]{1,0:T(8,128)(2,1)S(1)}, u32[]{:S(2)}, u32[]{:S(2)}) collective-permute-start(bf16[8,128]{1,0:T(8,128)(2,1)S(1)} %collective-permute-done.14), channel_id=1, source_target_pairs={{0,1},{1,2},{2,3},{3,0},{4,5},{5,6},{6,7},{7,4},{8,9},{9,10},{10,1... | collective-permute-start | bytes 6152 | tf_op jit(solution)/shard_map/ppermute | solution.py:48
  121.5 3.8 %collective-permute-start.17 = (bf16[32,128]{1,0:T(8,128)(2,1)S(1)}, bf16[32,128]{1,0:T(8,128)(2,1)S(1)}, u32[]{:S(2)}, u32[]{:S(2)}) collective-permute-start(bf16[32,128]{1,0:T(8,128)(2,1)S(1)} %constant_dynamic-update-slice_fusion.8), channel_id=1, source_target_pairs={{0,4},{4,0},{8,12},{12,8},{16,20},{20,16},{24,28},{28,24},{1,5},{5... | collective-permute-start | bytes 24584 | tf_op jit(solution)/shard_map/ppermute | solution.py:17
  125.3 13.5 %collective-permute-start.22 = (bf16[2048,128]{1,0:T(8,128)(2,1)}, bf16[2048,128]{1,0:T(8,128)(2,1)S(1)}, u32[]{:S(2)}, u32[]{:S(2)}) collective-permute-start(bf16[2048,128]{1,0:T(8,128)(2,1)} %constant_dynamic-update-slice_fusion.4), channel_id=1, source_target_pairs={{0,4},{4,0},{8,12},{12,8},{16,20},{20,16},{24,28},{28,24},{1,5},{5... | collective-permute-start | bytes 1572872 | tf_op jit(solution)/shard_map/ppermute | solution.py:17
  125.4 5.3 %collective-permute-start.18 = (bf16[64,128]{1,0:T(8,128)(2,1)S(1)}, bf16[64,128]{1,0:T(8,128)(2,1)S(1)}, u32[]{:S(2)}, u32[]{:S(2)}) collective-permute-start(bf16[64,128]{1,0:T(8,128)(2,1)S(1)} %pad_maximum_fusion.5), channel_id=1, source_target_pairs={{0,8},{8,0},{4,12},{12,4},{16,24},{24,16},{20,28},{28,20},{1,9},{9... | collective-permute-start | bytes 49160 | tf_op jit(solution)/shard_map/ppermute | solution.py:17
  131.8 10.1 %copy-start.6 = (bf16[512,64]{0,1:T(8,128)(2,1)S(1)}, bf16[512,64]{0,1:T(8,128)(2,1)}, u32[]{:S(2)}) copy-start(bf16[512,64]{0,1:T(8,128)(2,1)} %param.13) | copy-start | bytes 196612
  132.1 3.1 %collective-permute-start.23 = (bf16[8,128]{1,0:T(8,128)(2,1)S(1)}, bf16[8,128]{1,0:T(8,128)(2,1)S(1)}, u32[]{:S(2)}, u32[]{:S(2)}) collective-permute-start(bf16[8,128]{1,0:T(8,128)(2,1)S(1)} %get-tuple-element.8), channel_id=1, source_target_pairs={{0,1},{1,2},{2,3},{3,0},{4,5},{5,6},{6,7},{7,4},{8,9},{9,10},{10,1... | collective-permute-start | bytes 6152 | tf_op jit(solution)/shard_map/ppermute | solution.py:48
  132.2 3.0 %collective-permute-start.24 = (bf16[8,128]{1,0:T(8,128)(2,1)S(1)}, bf16[8,128]{1,0:T(8,128)(2,1)S(1)}, u32[]{:S(2)}, u32[]{:S(2)}) collective-permute-start(bf16[8,128]{1,0:T(8,128)(2,1)S(1)} %get-tuple-element.8), channel_id=1, source_target_pairs={{0,3},{1,0},{2,1},{3,2},{4,7},{5,4},{6,5},{7,6},{8,11},{9,8},{10,9... | collective-permute-start | bytes 6152 | tf_op jit(solution)/shard_map/ppermute | solution.py:53
  135.2 3.0 %collective-permute-start.25 = (bf16[8,128]{1,0:T(8,128)(2,1)S(1)}, bf16[8,128]{1,0:T(8,128)(2,1)S(1)}, u32[]{:S(2)}, u32[]{:S(2)}) collective-permute-start(bf16[8,128]{1,0:T(8,128)(2,1)S(1)} %collective-permute-done.23), channel_id=1, source_target_pairs={{0,1},{1,2},{2,3},{3,0},{4,5},{5,6},{6,7},{7,4},{8,9},{9,10},{10,1... | collective-permute-start | bytes 6152 | tf_op jit(solution)/shard_map/ppermute | solution.py:48
  138.2 3.7 %collective-permute-start.26 = (bf16[32,128]{1,0:T(8,128)(2,1)S(1)}, bf16[32,128]{1,0:T(8,128)(2,1)S(1)}, u32[]{:S(2)}, u32[]{:S(2)}) collective-permute-start(bf16[32,128]{1,0:T(8,128)(2,1)S(1)} %constant_dynamic-update-slice_fusion), channel_id=1, source_target_pairs={{0,4},{4,0},{8,12},{12,8},{16,20},{20,16},{24,28},{28,24},{1,5},{5... | collective-permute-start | bytes 24584 | tf_op jit(solution)/shard_map/ppermute | solution.py:17
